TPU v7x, 512 devices: a whole 4x8x8 slice. The times are simulated.
512 devices in a mesh: ens: 16 (over z, core), space: 32 (over y, x).
Axes of the slice: x: 4, y: 8, z: 8, core: 2. Of those that a mesh axis runs over, the one named last changes fastest.
Arguments:
- mesh_latent: bfloat16 [16, 4096, 512], P('ens', 'space'), may hold values from -6 to 6
- grid_embed: bfloat16 [16384, 512], P('space'), may hold values from -6 to 6
- w_send: bfloat16 [512, 512], replicated, may hold values from -0.25 to 0.25
- w_recv: bfloat16 [512, 512], replicated, may hold values from -0.25 to 0.25
- w_msg: bfloat16 [512, 512], replicated, may hold values from -0.25 to 0.25
- w_node: bfloat16 [512, 512], replicated, may hold values from -0.25 to 0.25
- w_out: bfloat16 [512, 100], replicated, may hold values from -0.25 to 0.25
- target: float32 [16384, 100], P('space'), may hold values from -6 to 6
- var_weight: float32 [100], replicated, may hold values from 0.5 to 4
- send_rows: int32 [32, 32, 8], P('space'), may hold values from 0 to 127
- edge_slot: int32 [16384, 4], P('space'), may hold values from 0 to 255
- edge_count: int32 [16384], P('space'), may hold values from 1 to 4
Outputs:
- mesh_grad: float32 [16, 4096, 512], P('ens', 'space')
- weight_grad: float32 [512, 512], P('space')
Inputs may be any that keep to these rules, and one draw needn't show every extreme that they name: `send_rows`: local mesh row indices of the sending index of space. `edge_slot`: slots index the receiving device's 32 * 8 received rows, sender-major.
All inputs are finite; a program needn't handle non-finite values.
Results may differ from a plain program's by a relative error of at most 0.013.
Values may be sent and summed in bfloat16 or wider, within the bound.
A program may use at most 64 MiB of HBM per device.

v0:
```python
import math

import jax
import jax.numpy as jnp
from jax import lax
from jax.sharding import PartitionSpec as P

soft_square = 0.09


def silu_grad(value):
    logistic = jax.nn.sigmoid(value)
    return logistic * (1.0 + value * (1.0 - logistic))


def crps_grad(mine, others, goal, var_weight):
    members = others.shape[0]
    spread = mine[None] - others
    pairwise = jnp.sum(spread / jnp.sqrt(spread * spread + soft_square), axis=0)
    target_gap = mine - goal
    return var_weight * (
        target_gap / jnp.sqrt(target_gap * target_gap + soft_square) - pairwise / (members - 1.0)
    )


def body(
    mesh_latent,
    grid_embed,
    w_send,
    w_recv,
    w_msg,
    w_node,
    w_out,
    target,
    var_weight,
    send_rows,
    edge_slot,
    edge_count,
):
    latent = mesh_latent[0]
    features = grid_embed.shape[1]
    points = grid_embed.shape[0]
    per_point = edge_slot.shape[1]
    per_peer = send_rows.shape[2]
    nspace = lax.axis_size("space")
    local_rows = latent.shape[0]
    wanted = send_rows[0].reshape(-1)
    picked = jnp.take(latent, wanted, axis=0).reshape(nspace, per_peer, features)
    arrived = lax.all_to_all(picked, "space", split_axis=0, concat_axis=0, tiled=True)
    slot_proj = jnp.dot(arrived.reshape(-1, features), w_send, preferred_element_type=jnp.float32)
    grid_proj = jnp.dot(grid_embed, w_recv, preferred_element_type=jnp.float32)
    live_mask = (jnp.arange(per_point, dtype=jnp.int32)[None, :] < edge_count[:, None]).astype(
        jnp.float32
    )
    preact = (
        jnp.take(slot_proj, edge_slot.reshape(-1), axis=0).reshape(points, per_point, features)
        + grid_proj[:, None, :]
    )
    activation = jax.nn.silu(preact).astype(jnp.bfloat16).reshape(-1, features)
    messages = jnp.dot(activation, w_msg, preferred_element_type=jnp.float32).reshape(
        points, per_point, features
    )
    summed = jnp.sum(messages * live_mask[:, :, None], axis=1)
    node_in = (summed + grid_embed.astype(jnp.float32)).astype(jnp.bfloat16)
    node_pre = jnp.dot(node_in, w_node, preferred_element_type=jnp.float32)
    hidden = jax.nn.silu(node_pre).astype(jnp.bfloat16)
    pred = jnp.dot(hidden, w_out, preferred_element_type=jnp.float32)
    every = lax.all_gather(pred[None], "ens", axis=0, tiled=True)
    members = every.shape[0]
    pred_grad = crps_grad(pred, every, target, var_weight).astype(jnp.bfloat16)
    hidden_grad = (
        jnp.dot(pred_grad, w_out.T, preferred_element_type=jnp.float32) * silu_grad(node_pre)
    ).astype(jnp.bfloat16)
    edge_grad = jnp.dot(hidden_grad, w_node.T, preferred_element_type=jnp.float32).astype(
        jnp.bfloat16
    )
    message_grad = (
        (edge_grad[:, None, :].astype(jnp.float32) * live_mask[:, :, None])
        .astype(jnp.bfloat16)
        .reshape(-1, features)
    )
    preact_grad = (
        jnp.dot(message_grad, w_msg.T, preferred_element_type=jnp.float32).reshape(
            points, per_point, features
        )
        * silu_grad(preact)
    ).astype(jnp.bfloat16)
    scattered = lax.psum_scatter(
        lax.dot_general(
            activation, message_grad, (((0,), (0,)), ((), ())), preferred_element_type=jnp.float32
        ).astype(jnp.bfloat16),
        "space",
        scatter_dimension=0,
        tiled=True,
    )
    total_grid = points * nspace
    weight_grad = lax.psum(scattered, "ens").astype(jnp.float32) * (
        1.0 / math.sqrt(members * total_grid * per_point)
    )
    slot_grad = jax.ops.segment_sum(
        preact_grad.reshape(-1, features).astype(jnp.float32),
        edge_slot.reshape(-1),
        num_segments=nspace * per_peer,
    )
    w_send_wide = w_send.astype(jnp.float32)
    outgoing = jnp.dot(slot_grad, w_send_wide.T, precision=lax.Precision.HIGHEST)
    incoming = lax.all_to_all(
        outgoing.reshape(nspace, per_peer, features).astype(jnp.bfloat16),
        "space",
        split_axis=0,
        concat_axis=0,
        tiled=True,
    ).astype(jnp.float32)
    row_grads = jax.ops.segment_sum(incoming.reshape(-1, features), wanted, num_segments=local_rows)
    return (row_grads[None], weight_grad)


def solution(mesh):
    in_specs = (
        P("ens", "space", None),
        P("space", None),
        P(),
        P(),
        P(),
        P(),
        P(),
        P("space", None),
        P(),
        P("space", None, None),
        P("space", None),
        P("space"),
    )
    out_specs = (P("ens", "space", None), P("space", None))
    return jax.shard_map(body, mesh=mesh, in_specs=in_specs, out_specs=out_specs, check_vma=False)
```

profile of v0, /device:TPU:1, one launch (start us, length us, event | category | flops | bytes accessed | tf_op | source)
XLA Modules:
  0.0 383.8 jit_solution(14121411469162930136)
XLA Ops:
  7.2 0.0 copy-start
  7.2 0.0 copy-start.3
  7.2 0.8 compare_and_fusion.1
  8.0 0.8 copy.16
  8.8 0.1 copy.18
  8.9 0.1 broadcast_in_dim_reshape_squeeze.3
  9.0 2.1 gather_fusion
  11.1 0.8 bitcast_select_fusion
  11.9 10.6 %all-to-all-start = ((bf16[32,8,512]{2,1,0:T(8,128)(2,1)}), bf16[32,8,512]{2,1,0:T(8,128)(2,1)}, u32[]{:S(2)}, u32[]{:S(2)}) async-start(bf16[32,8,512]{2,1,0:T(8,128)(2,1)} %bitcast_select_fusion), calls=%async_computation | async-start | bytes 524288 | tf_op jit(solution)/shard_map/all_to_all | solution.py:49
  22.6 0.0 all-gather.3.cloned.1.call-start
  22.6 0.8 copy.17
  23.5 0.2 broadcast_in_dim_reshape.3
  23.7 0.7 fusion.36
  24.4 1.5 fusion.43
  25.9 7.8 %all-to-all-done = bf16[32,8,512]{2,1,0:T(8,128)(2,1)} async-done(((bf16[32,8,512]{2,1,0:T(8,128)(2,1)}), bf16[32,8,512]{2,1,0:T(8,128)(2,1)}, u32[]{:S(2)}, u32[]{:S(2)}) %all-to-all-start) | async-done | bytes 262176 | tf_op jit(solution)/shard_map/all_to_all | solution.py:49
  33.7 1.2 fusion.25
  35.0 9.0 %gather_fusion.1 = f32[2048,512]{1,0:T(8,128)} fusion(f32[256,512]{1,0:T(8,128)S(1)} %fusion.25, s32[2048]{0:T(1024)S(1)} %broadcast_clamp_fusion), kind=kCustom, calls=%fused_computation.1 | custom fusion | bytes 8396800 | tf_op jit(solution)/shard_map/jit(_take)/gather | solution.py:56
  44.0 5.2 %gather.15 = f32[512,4,512]{2,1,0:T(4,128)} reshape(f32[2048,512]{1,0:T(8,128)} %gather_fusion.1) | data formatting | bytes 8388608 | tf_op jit(solution)/shard_map/jit(_take)/gather | solution.py:56
  49.1 4.0 %multiply_convert_fusion.2 = bf16[512,4,512]{2,0,1:T(8,128)(2,1)S(1)} fusion(f32[512,4,512]{2,1,0:T(4,128)} %gather.15, f32[512,512]{1,0:T(8,128)S(1)} %fusion.43, pred[512,4]{0,1:T(4,128)(4,1)S(1)} %get-tuple-element.3), kind=kLoop, calls=%fused_computation.9 | loop fusion | flops 7340032 | bytes 7342080 | tf_op jit(solution)/shard_map/convert_element_type | solution.py:59
  53.1 0.0 copy-start.6
  53.1 0.0 copy-start.9
  53.2 1.3 multiply_reduce_fusion
  54.4 0.1 copy-done.6
  54.5 0.4 fusion.17
  55.0 1.0 copy-done.4
  56.0 0.0 copy-done.9
  56.0 1.1 fusion.23
  57.1 0.0 all-gather.3.cloned.1.call-update
  57.2 0.0 reduce-scatter.2.cloned.1.call-start
  57.2 0.2 reshape.171
  57.4 45.7 %all-gather.3.cloned.1.call-done = f32[8192,100]{0,1:T(8,128)} async-done(((f32[512,100]{0,1:T(8,128)}), f32[8192,100]{0,1:T(8,128)}) %all-gather.3.cloned.1.call-update) | async-done | bytes 3276816 | tf_op jit(solution)/shard_map/all_gather | solution.py:68
  103.0 4.5 %copy.25 = f32[13,8,16,512]{3,2,1,0:T(8,128)S(1)} copy(f32[13,8,16,512]{3,1,2,0:T(8,128)} %bitcast.51) | data formatting | bytes 6815744
  107.5 1.2 multiply_reduce_fusion.1
  108.7 3.0 fusion.10
  111.8 4.0 %fusion.11 = bf16[512,512]{1,0:T(8,128)(2,1)} fusion(bf16[512,4,512]{2,0,1:T(8,128)(2,1)} %copy-done.2, f32[512,512]{1,0:T(8,128)} %fusion.10, f32[512,4]{0,1:T(4,128)S(1)} %get-tuple-element.2), kind=kOutput, calls=%fused_computation.25 | convolution fusion | flops 1076101120 | bytes 3678208 | tf_op jit(solution)/shard_map/dot_general | solution.py:89
  115.7 0.0 reduce-scatter.2.cloned.1.call-update
  115.8 5.6 %fusion.7 = f32[512,4,512]{2,0,1:T(8,128)S(1)} fusion(f32[512,512]{1,0:T(8,128)S(1)} %fusion.43, f32[512,4,512]{2,1,0:T(4,128)} %gather.15, pred[512,4]{0,1:T(4,128)(4,1)S(1)} %get-tuple-element.3, f32[512,512]{1,0:T(8,128)} %fusion.10, f32[512,4]{0,1:T(4,128)S(1)} %get-tuple-element.2, bf16[512,512]{1,0:T(8,128)(2,1)S(1)} %copy-done), kind=kOutput, calls=%fused_computation.19 | convolution fusion | flops 1088421888 | bytes 11020288 | tf_op jit(solution)/shard_map/dot_general | solution.py:83
  121.4 4.6 %copy.22 = f32[512,4,512]{2,1,0:T(4,128)} copy(f32[512,4,512]{2,0,1:T(8,128)S(1)} %fusion.7) | data formatting | bytes 8388608 | tf_op jit(solution)/shard_map/convert_element_type | solution.py:101
  126.0 5.3 %reshape.173 = f32[2048,512]{1,0:T(8,128)} reshape(f32[512,4,512]{2,1,0:T(4,128)} %copy.22) | data formatting | bytes 8388608 | tf_op jit(solution)/shard_map/convert_element_type | solution.py:101
  131.3 13.4 %scatter_custom_fusion = f32[256,512]{1,0:T(8,128)S(1)} fusion(s32[2048]{0:T(1024)S(1)} %reshape.171, f32[2048,512]{1,0:T(8,128)} %reshape.173, f32[]{:T(128)} %constant.21.clone.1), kind=kCustom, calls=%fused_computation.46 | custom fusion | flops 1048576 | bytes 524800 | tf_op jit(solution)/shard_map/scatter-add | solution.py:100
  144.7 1.3 fusion.12
  146.0 9.3 %all-to-all-start.1 = ((bf16[32,8,512]{2,1,0:T(8,128)(2,1)}), bf16[32,8,512]{2,1,0:T(8,128)(2,1)S(1)}, u32[]{:S(2)}, u32[]{:S(2)}) async-start(bf16[32,8,512]{2,1,0:T(8,128)(2,1)} %fusion.12), calls=%async_computation.1 | async-start | bytes 524288 | tf_op jit(solution)/shard_map/all_to_all | solution.py:107
  155.3 0.1 reshape.179
  155.4 11.8 %all-to-all-done.1 = bf16[32,8,512]{2,1,0:T(8,128)(2,1)S(1)} async-done(((bf16[32,8,512]{2,1,0:T(8,128)(2,1)}), bf16[32,8,512]{2,1,0:T(8,128)(2,1)S(1)}, u32[]{:S(2)}, u32[]{:S(2)}) %all-to-all-start.1) | async-done | bytes 262176 | tf_op jit(solution)/shard_map/all_to_all | solution.py:107
  167.2 2.8 scatter_custom_fusion.1
  170.0 157.3 %reduce-scatter.2.cloned.1.call-done = bf16[16,512]{1,0:T(8,128)(2,1)} async-done(((bf16[512,512]{1,0:T(8,128)(2,1)}), bf16[16,512]{1,0:T(8,128)(2,1)}) %reduce-scatter.2.cloned.1.call-update) | async-done | bytes 16400 | tf_op jit(solution)/shard_map/reduce_scatter | solution.py:88
  327.4 49.0 %psum.7 = bf16[16,512]{1,0:T(8,128)(2,1)S(1)} all-reduce(bf16[16,512]{1,0:T(8,128)(2,1)} %reduce-scatter.2.cloned.1.call-done), channel_id=1, replica_groups=mesh['ens'=16,'space'=32] {'ens'}, use_global_device_ids=true, to_apply=%region_5.6 | all-reduce | flops 8192 | bytes 32768 | tf_op jit(solution)/shard_map/psum | solution.py:97
  376.4 0.6 convert_multiply_fusion
  (19 shorter events, 0.1 us)
Async XLA Ops:
  7.2 46.0 %copy-start = (bf16[512,512]{1,0:T(8,128)(2,1)S(1)}, bf16[512,512]{1,0:T(8,128)(2,1)}, u32[]{:S(2)}) copy-start(bf16[512,512]{1,0:T(8,128)(2,1)} %param.16) | copy-start | bytes 1572868
  7.2 17.2 %copy-start.3 = (bf16[512,512]{1,0:T(8,128)(2,1)S(1)}, bf16[512,512]{1,0:T(8,128)(2,1)}, u32[]{:S(2)}) copy-start(bf16[512,512]{1,0:T(8,128)(2,1)} %param.13) | copy-start | bytes 1572868
  7.2 26.5 %copy-start.1 = (bf16[512,512]{1,0:T(8,128)(2,1)S(1)}, bf16[512,512]{1,0:T(8,128)(2,1)}, u32[]{:S(2)}) copy-start(bf16[512,512]{1,0:T(8,128)(2,1)} %param.14) | copy-start | bytes 1572868
  11.9 21.8 %all-to-all-start = ((bf16[32,8,512]{2,1,0:T(8,128)(2,1)}), bf16[32,8,512]{2,1,0:T(8,128)(2,1)}, u32[]{:S(2)}, u32[]{:S(2)}) async-start(bf16[32,8,512]{2,1,0:T(8,128)(2,1)} %bitcast_select_fusion), calls=%async_computation | async-start | bytes 524288 | tf_op jit(solution)/shard_map/all_to_all | solution.py:49
  22.6 80.5 %all-gather.3.cloned.1.call-start = ((), (), s32[]{:S(2)}) async-start(), calls=%async_computation.4 | async-start | bytes 3620864 | tf_op jit(solution)/shard_map/all_gather | solution.py:68
  53.1 1.9 copy-start.2
  53.1 1.4 copy-start.6
  53.1 2.9 copy-start.9
  55.0 1.0 copy-start.4
  57.1 50.4 %copy-start.5 = (f32[512,100]{0,1:T(8,128)S(1)}, f32[512,100]{0,1:T(8,128)}, u32[]{:S(2)}) copy-start(f32[512,100]{0,1:T(8,128)} %fusion.23) | copy-start | bytes 614404
  57.2 270.2 %reduce-scatter.2.cloned.1.call-start = ((), (), s32[]{:S(2)}) async-start(), calls=%async_computation.3 | async-start | bytes 540672 | tf_op jit(solution)/shard_map/reduce_scatter | solution.py:88
  103.0 5.7 %copy-start.7 = (bf16[512,512]{1,0:T(8,128)(2,1)S(1)}, bf16[512,512]{1,0:T(8,128)(2,1)}, u32[]{:S(2)}) copy-start(bf16[512,512]{1,0:T(8,128)(2,1)} %param.17) | copy-start | bytes 1572868
  103.0 5.7 %copy-start.8 = (f32[512,100]{0,1:T(8,128)S(1)}, f32[512,100]{0,1:T(8,128)}, u32[]{:S(2)}) copy-start(f32[512,100]{0,1:T(8,128)} %param.19) | copy-start | bytes 614404
  103.0 5.7 %copy-start.10 = (f32[100]{0:T(128)S(1)}, f32[100]{0:T(128)}, u32[]{:S(2)}) copy-start(f32[100]{0:T(128)} %param.20) | copy-start | bytes 1204
  146.0 21.2 %all-to-all-start.1 = ((bf16[32,8,512]{2,1,0:T(8,128)(2,1)}), bf16[32,8,512]{2,1,0:T(8,128)(2,1)S(1)}, u32[]{:S(2)}, u32[]{:S(2)}) async-start(bf16[32,8,512]{2,1,0:T(8,128)(2,1)} %fusion.12), calls=%async_computation.1 | async-start | bytes 524288 | tf_op jit(solution)/shard_map/all_to_all | solution.py:107
Sparse Core Ops, SparseCore 0:
  57.3 45.7 all-gather.2
  115.9 211.4 reduce-scatter.1
where the time goes:
time: 386 us; the launch traced here: 384 us
  waiting for transfers between devices  223 us (58%)
  blocking collectives  49 us (13%)
  local copies, waits for them, and re-layouts  34 us (9%)
  other arithmetic  24.3 us (6%)
  starting transfers between devices  20 us (5%)
  matrix products  19.5 us (5%)
  between operations  14.3 us (4%)
    reduce_scatter x1, waiting for transfers between devices, body(): lax.psum_scatter(lax.dot_general(activation, message_grad, (((0,), (0,)),...  157 us
    psum x1, blocking collectives, body(): lax.psum(scattered, 'ens').astype(jnp.float32)  49 us
    all_gather x1, waiting for transfers between devices, body(): every = lax.all_gather(pred[None], 'ens', axis=0, tiled=True)  45.7 us
    gather x2, local copies, waits for them, and re-layouts, body(): jnp.take(slot_proj, edge_slot.reshape(-1), axis=0)  14.1 us
    scatter-add x1, other arithmetic, body(): jax.ops.segment_sum(preact_grad.reshape(-1, features).astype(jnp.float32)...  13.4 us
    all_to_all x1, waiting for transfers between devices, body(): lax.all_to_all(outgoing.reshape(nspace, per_peer, features).astype(jnp.bf...  11.8 us
    all_to_all x1, starting transfers between devices, body(): lax.all_to_all(picked, 'space', split_axis=0, concat_axis=0, tiled=True)  10.6 us
    convert_element_type x2, local copies, waits for them, and re-layouts, body(): preact_grad.reshape(-1, features).astype(jnp.float32)  9.94 us
  transfers between devices with their start and end apart: 4, of which 4 were waited for; matrix products, arithmetic and copies ran while one was open for 10% of the time, Pallas kernels for 0%

commit v1 on v0

v1 whole, which is shorter than its diff:
```python
import functools
import math

import jax
import jax.numpy as jnp
from jax import lax
from jax.experimental import pallas as pl
from jax.experimental.pallas import tpu as pltpu
from jax.sharding import PartitionSpec as P

MESH = pl.DeviceIdType.MESH
F32 = jnp.float32
BF16 = jnp.bfloat16
SOFT = 0.09
LANES = 128


def sigmoid(v):
    return 0.5 * jnp.tanh(0.5 * v) + 0.5


def dot(a, b):
    return jnp.dot(a, b, preferred_element_type=F32)


def dot_t(a, b):
    return lax.dot_general(a, b, (((1,), (1,)), ((), ())), preferred_element_type=F32)


def to_blocks(rows, n):
    c, f = rows.shape[0] // n, rows.shape[1]
    split = rows.reshape(n, c, f)
    return jnp.concatenate([split[:, :, : f // 2], split[:, :, f // 2 :]], axis=1)


def from_blocks(blocks):
    n, c2, f2 = blocks.shape
    c = c2 // 2
    left = blocks[:, :c, :].reshape(n * c, f2)
    right = blocks[:, c:, :].reshape(n * c, f2)
    return jnp.concatenate([left, right], axis=1)


def kernel(
    n_ens,
    n_sp,
    scale,
    lat_h,
    emb_h,
    w_send_h,
    w_recv_h,
    w_msg_h,
    w_node_h,
    w_out_h,
    target_h,
    var_ref,
    rows_ref,
    slot_ref,
    count_ref,
    mesh_ref,
    weight_ref,
    lat,
    emb,
    w_send,
    w_recv,
    w_msg,
    w_node,
    w_out_raw,
    target_raw,
    w_out_wide,
    w_out,
    target_wide,
    target,
    small,
    columns,
    pick,
    pick_t,
    out_rows,
    in_rows,
    slot_proj,
    grid_proj,
    one_hot,
    one_hot_t,
    pre,
    live,
    summed_act,
    summed_act_t,
    node_pre,
    pred,
    pred_in,
    grad_wide,
    grad_out,
    grad_in,
    pred_grad,
    edge_grad,
    back,
    pre_grad,
    own_half,
    pair_out,
    pair_in,
    z_out,
    z_in,
    part_out,
    part_in,
    total_out,
    total_in,
    rows_out,
    rows_in,
    load_sem,
    send_sem,
    recv_sem,
):
    ens = lax.axis_index("ens")
    sp = lax.axis_index("space")
    n_z = n_ens // 2
    core = lax.rem(ens, 2)
    z = lax.div(ens, 2)
    points, features = emb.shape
    per_point = slot_ref.shape[0]
    cap = rows_ref.shape[0]
    slots = n_sp * cap
    chunk = points // n_ens
    half = features // 2
    block = features // n_ens
    out_block = features // n_sp
    per_block = n_sp // n_ens

    loads = [
        pltpu.make_async_copy(src, dst, load_sem.at[i])
        for i, (src, dst) in enumerate(
            [
                (lat_h, lat),
                (emb_h, emb),
                (w_recv_h, w_recv),
                (w_send_h, w_send),
                (w_msg_h, w_msg),
                (w_node_h, w_node),
                (w_out_h, w_out_raw),
                (target_h, target_raw),
            ]
        )
    ]
    for load in loads:
        load.start()

    barrier = pltpu.get_barrier_semaphore()

    @pl.loop(1, n_sp)
    def _(q):
        pl.semaphore_signal(
            barrier, inc=1, device_id={"space": lax.rem(sp + q, n_sp)}, device_id_type=MESH
        )

    @pl.loop(1, n_ens)
    def _(q):
        pl.semaphore_signal(
            barrier, inc=1, device_id={"ens": lax.rem(ens + q, n_ens)}, device_id_type=MESH
        )

    def exchange(src, dst, which, axis, me, n):
        @pl.loop(1, n)
        def _(q):
            pltpu.make_async_remote_copy(
                src_ref=src.at[q],
                dst_ref=dst.at[n - q],
                send_sem=send_sem.at[which],
                recv_sem=recv_sem.at[which],
                device_id={axis: lax.rem(me + q, n)},
                device_id_type=MESH,
            ).start()

    def whole(ref, which):
        return pltpu.make_async_remote_copy(
            src_ref=ref,
            dst_ref=ref,
            send_sem=send_sem.at[which],
            recv_sem=recv_sem.at[which],
            device_id={"ens": ens},
            device_id_type=MESH,
        )

    tiled = jnp.broadcast_to(
        rows_ref[...].astype(F32)[None], (n_sp, cap, n_sp)
    ).reshape(slots, n_sp)
    place = lax.broadcasted_iota(jnp.int32, (slots, n_sp), 0) // cap + sp
    place = jnp.where(place >= n_sp, place - n_sp, place)
    lane = lax.broadcasted_iota(jnp.int32, (slots, n_sp), 1)
    wanted = jnp.sum(jnp.where(lane == place, tiled, 0.0), axis=1, keepdims=True)
    local_rows = lat.shape[0]
    pick_wide = jnp.where(
        lax.broadcasted_iota(jnp.int32, (slots, local_rows), 1).astype(F32) == wanted, 1.0, 0.0
    )
    pick[...] = pick_wide.astype(BF16)
    loads[0].wait()
    blocks = to_blocks(dot(pick[...], lat[...]), n_sp).astype(BF16)
    out_rows[...] = blocks
    in_rows[0] = blocks[0]
    pl.semaphore_wait(barrier, n_sp + n_ens - 2)
    exchange(out_rows, in_rows, 0, "space", sp, n_sp)

    loads[1].wait()
    loads[2].wait()
    grid_proj[...] = dot(emb[...], w_recv[...])
    pick_t[...] = jnp.transpose(pick_wide).astype(BF16)
    slot = slot_ref[...] - cap * sp
    slot = jnp.where(slot < 0, slot + slots, slot)
    is_live = lax.broadcasted_iota(jnp.int32, slot.shape, 0) < count_ref[...]
    small[...] = jnp.zeros_like(small)
    small[0:per_point, :] = slot.astype(F32)
    small[per_point : 2 * per_point, :] = jnp.where(is_live, 1.0, 0.0)
    columns[...] = jnp.transpose(small[...])
    slot = jnp.where(is_live, slot, -1)
    slot_index = lax.broadcasted_iota(jnp.int32, (slots, points), 0)
    lane_index = lax.broadcasted_iota(jnp.int32, (points, slots), 1).astype(F32)
    for k in range(per_point):
        one_hot[k] = jnp.where(lane_index == columns[:, k : k + 1], 1.0, 0.0).astype(BF16)
        one_hot_t[:, k * points : (k + 1) * points] = jnp.where(
            slot_index == slot[k : k + 1, :], 1.0, 0.0
        ).astype(BF16)
        live[k] = jnp.broadcast_to(
            columns[:, per_point + k : per_point + k + 1], (points, LANES)
        )
    loads[6].wait()
    variables = w_out_raw.shape[0]
    w_out_wide[...] = jnp.zeros_like(w_out_wide)
    w_out_wide[0:variables, :] = w_out_raw[...].astype(F32)
    w_out[...] = w_out_wide[...].astype(BF16)
    loads[7].wait()
    target_wide[...] = jnp.zeros_like(target_wide)
    target_wide[0:variables, :] = target_raw[...]
    target[...] = jnp.transpose(target_wide[...])
    loads[3].wait()
    loads[4].wait()
    loads[5].wait()

    whole(in_rows.at[pl.ds(1, n_sp - 1)], 0).wait_recv()
    arrived = from_blocks(in_rows[...].astype(F32)).astype(BF16)
    slot_proj[...] = dot(arrived, w_send[...]).astype(BF16)
    for k in range(per_point):
        pre[k] = dot(one_hot[k], slot_proj[...])

    step = 16

    def spread(k, rows):
        return jnp.concatenate([live[k, rows, :]] * (features // LANES), axis=1)

    @pl.loop(0, points // step)
    def _(i):
        rows = pl.ds(pl.multiple_of(i * step, step), step)
        base = grid_proj[rows, :]
        total = jnp.zeros((step, features), F32)
        for k in range(per_point):
            v = pre[k, rows, :] + base
            total += v * sigmoid(v) * spread(k, rows)
        summed_act[rows, :] = total.astype(BF16)

    node_in = (dot(summed_act[...], w_msg[...]) + emb[...].astype(F32)).astype(BF16)
    node_pre[...] = dot(node_in, w_node[...])
    v = node_pre[...]
    hidden = (v * sigmoid(v)).astype(BF16)
    pred[...] = dot_t(hidden, w_out[...]).reshape(pred.shape)

    pred_in[0] = pred[ens]

    @pl.loop(1, n_ens)
    def _(q):
        to = lax.rem(ens + q, n_ens)
        pltpu.make_async_remote_copy(
            src_ref=pred.at[to],
            dst_ref=pred_in.at[n_ens - q],
            send_sem=send_sem.at[1],
            recv_sem=recv_sem.at[1],
            device_id={"ens": to},
            device_id_type=MESH,
        ).start()

    @pl.loop(0, points // step)
    def _(i):
        rows = pl.ds(pl.multiple_of(i * step, step), step)
        base = grid_proj[rows, :]
        for k in range(per_point):
            v = pre[k, rows, :] + base
            s = sigmoid(v)
            pre[k, rows, :] = s * (1.0 + v * (1.0 - s))
        v = node_pre[rows, :]
        s = sigmoid(v)
        node_pre[rows, :] = s * (1.0 + v * (1.0 - s))

    summed_act_t[...] = jnp.transpose(summed_act[...].astype(F32)).astype(BF16)

    whole(pred_in.at[pl.ds(1, n_ens - 1)], 1).wait_recv()
    weight_row = var_ref[...]

    @pl.loop(0, chunk // 8)
    def _(i):
        rows = pl.ds(pl.multiple_of(i * 8, 8), 8)
        goal = target[pl.ds(pl.multiple_of(ens * chunk + i * 8, 8), 8), :]
        mine = [pred_in[m, rows, :] for m in range(n_ens)]
        pairwise = [jnp.zeros_like(goal) for _ in range(n_ens)]
        for a in range(n_ens):
            for b in range(a + 1, n_ens):
                t = mine[a] - mine[b]
                g = t * lax.rsqrt(t * t + SOFT)
                pairwise[a] += g
                pairwise[b] -= g
        for m in range(n_ens):
            t = mine[m] - goal
            g = t * lax.rsqrt(t * t + SOFT)
            grad_wide[m, rows, :] = weight_row * (g - pairwise[m] * (1.0 / (n_ens - 1.0)))

    grad_out[...] = grad_wide[...].astype(BF16)
    grad_in[0] = grad_out[0]
    exchange(grad_out, grad_in, 2, "ens", ens, n_ens)
    whole(grad_in.at[pl.ds(1, n_ens - 1)], 2).wait_recv()

    @pl.loop(0, n_ens)
    def _(q):
        pred_grad[lax.rem(ens + q, n_ens)] = grad_in[q]

    hidden_grad = (
        dot(pred_grad[...].reshape(points, LANES), w_out[...]) * node_pre[...]
    ).astype(BF16)
    edge_grad[...] = dot_t(hidden_grad, w_node[...]).astype(BF16)

    theirs = pl.ds(pl.multiple_of((1 - core) * half, half), half)
    ours = pl.ds(pl.multiple_of(core * half, half), half)
    pair_out[...] = dot(summed_act_t[theirs, :], edge_grad[...]).astype(BF16)
    pair = pltpu.make_async_remote_copy(
        src_ref=pair_out,
        dst_ref=pair_in,
        send_sem=send_sem.at[3],
        recv_sem=recv_sem.at[3],
        device_id={"ens": ens + 1 - 2 * core},
        device_id_type=MESH,
    )
    pair.start()
    back[...] = dot_t(edge_grad[...], w_msg[...])
    own_half[...] = dot(summed_act_t[ours, :], edge_grad[...])
    pair.wait_recv()
    z_out[...] = (own_half[...] + pair_in[...].astype(F32)).astype(BF16).reshape(z_out.shape)
    z_in[0] = z_out[z]

    @pl.loop(1, n_z)
    def _(q):
        to = lax.rem(z + q, n_z)
        pltpu.make_async_remote_copy(
            src_ref=z_out.at[to],
            dst_ref=z_in.at[n_z - q],
            send_sem=send_sem.at[4],
            recv_sem=recv_sem.at[4],
            device_id={"ens": 2 * to + core},
            device_id_type=MESH,
        ).start()

    @pl.loop(0, points // step)
    def _(i):
        rows = pl.ds(pl.multiple_of(i * step, step), step)
        b = back[rows, :]
        for k in range(per_point):
            pre_grad[k, rows, :] = (b * pre[k, rows, :]).astype(BF16)

    slot_grad = dot(one_hot_t[...], pre_grad[...].reshape(per_point * points, features))
    blocks = to_blocks(slot_grad, n_sp).astype(BF16)
    rows_out[...] = blocks
    rows_in[0] = blocks[0]
    exchange(rows_out, rows_in, 5, "space", sp, n_sp)

    whole(z_in.at[pl.ds(1, n_z - 1)], 4).wait_recv()
    part = jnp.sum(z_in[...].astype(F32), axis=0)
    part_out[...] = part.astype(BF16).reshape(part_out.shape)
    index = core * n_z + z
    for i in range(per_block):
        to = index * per_block + i

        @pl.when(to != sp)
        def _():
            pltpu.make_async_remote_copy(
                src_ref=part_out.at[i],
                dst_ref=part_in.at[lax.rem(sp - to + n_sp, n_sp)],
                send_sem=send_sem.at[6],
                recv_sem=recv_sem.at[6],
                device_id={"space": to},
                device_id_type=MESH,
            ).start()

        @pl.when(to == sp)
        def _():
            part_in[0] = part_out[i]

    whole(rows_in.at[pl.ds(1, n_sp - 1)], 5).wait_recv()
    back_rows = from_blocks(rows_in[...].astype(F32)).astype(BF16)
    row_grads = dot(pick_t[...], back_rows)
    high = row_grads.astype(BF16)
    low = (row_grads - high.astype(F32)).astype(BF16)
    mesh_ref[...] = dot_t(high, w_send[...]) + dot_t(low, w_send[...])

    owner = lax.div(sp, per_block) == index

    @pl.when(owner)
    def _():
        whole(part_in.at[pl.ds(1, n_sp - 1)], 6).wait_recv()
        total = jnp.sum(part_in[...].astype(F32), axis=0)
        weight_ref[...] = total * scale
        total_out[...] = total.astype(BF16)

        @pl.loop(1, n_ens)
        def _(q):
            pltpu.make_async_remote_copy(
                src_ref=total_out,
                dst_ref=total_in,
                send_sem=send_sem.at[7],
                recv_sem=recv_sem.at[7],
                device_id={"ens": lax.rem(ens + q, n_ens)},
                device_id_type=MESH,
            ).start()

        @pl.loop(1, n_ens)
        def _(q):
            whole(total_out, 7).wait_send()

    @pl.when(jnp.logical_not(owner))
    def _():
        whole(total_in, 7).wait_recv()
        weight_ref[...] = total_in[...].astype(F32) * scale

    for i in range(per_block):

        @pl.when(index * per_block + i != sp)
        def _():
            whole(part_out.at[i], 6).wait_send()

    whole(out_rows.at[pl.ds(1, n_sp - 1)], 0).wait_send()
    whole(pred_in.at[pl.ds(1, n_ens - 1)], 1).wait_send()
    whole(grad_out.at[pl.ds(1, n_ens - 1)], 2).wait_send()
    pair.wait_send()
    whole(z_in.at[pl.ds(1, n_z - 1)], 4).wait_send()
    whole(rows_out.at[pl.ds(1, n_sp - 1)], 5).wait_send()


def body(
    n_ens,
    n_sp,
    mesh_latent,
    grid_embed,
    w_send,
    w_recv,
    w_msg,
    w_node,
    w_out,
    target,
    var_weight,
    send_rows,
    edge_slot,
    edge_count,
):
    local_rows, features = mesh_latent.shape[1:]
    points, per_point = edge_slot.shape
    variables = target.shape[1]
    cap = send_rows.shape[2]
    slots = n_sp * cap
    chunk = points // n_ens
    half = features // 2
    n_z = n_ens // 2
    out_block = features // n_sp
    per_block = n_sp // n_ens
    total = n_ens * points * n_sp * per_point
    hbm = pl.BlockSpec(memory_space=pl.ANY)
    vmem = pl.BlockSpec(memory_space=pltpu.VMEM)
    square = (features, features)
    rows_blocks = (n_sp, 2 * cap, half)
    scratch = [
        pltpu.VMEM((local_rows, features), BF16),
        pltpu.VMEM((points, features), BF16),
        pltpu.VMEM(square, BF16),
        pltpu.VMEM(square, BF16),
        pltpu.VMEM(square, BF16),
        pltpu.VMEM(square, BF16),
        pltpu.VMEM((variables, features), BF16),
        pltpu.VMEM((variables, points), F32),
        pltpu.VMEM((LANES, features), F32),
        pltpu.VMEM((LANES, features), BF16),
        pltpu.VMEM((LANES, points), F32),
        pltpu.VMEM((points, LANES), F32),
        pltpu.VMEM((LANES, points), F32),
        pltpu.VMEM((points, LANES), F32),
        pltpu.VMEM((slots, local_rows), BF16),
        pltpu.VMEM((local_rows, slots), BF16),
        pltpu.VMEM(rows_blocks, BF16),
        pltpu.VMEM(rows_blocks, BF16),
        pltpu.VMEM((slots, features), BF16),
        pltpu.VMEM((points, features), F32),
        pltpu.VMEM((per_point, points, slots), BF16),
        pltpu.VMEM((slots, per_point * points), BF16),
        pltpu.VMEM((per_point, points, features), F32),
        pltpu.VMEM((per_point, points, LANES), F32),
        pltpu.VMEM((points, features), BF16),
        pltpu.VMEM((features, points), BF16),
        pltpu.VMEM((points, features), F32),
        pltpu.VMEM((n_ens, chunk, LANES), F32),
        pltpu.VMEM((n_ens, chunk, LANES), F32),
        pltpu.VMEM((n_ens, chunk, LANES), F32),
        pltpu.VMEM((n_ens, chunk, LANES), BF16),
        pltpu.VMEM((n_ens, chunk, LANES), BF16),
        pltpu.VMEM((n_ens, chunk, LANES), BF16),
        pltpu.VMEM((points, features), BF16),
        pltpu.VMEM((points, features), F32),
        pltpu.VMEM((per_point, points, features), BF16),
        pltpu.VMEM((half, features), F32),
        pltpu.VMEM((half, features), BF16),
        pltpu.VMEM((half, features), BF16),
        pltpu.VMEM((n_z, features // n_ens, features), BF16),
        pltpu.VMEM((n_z, features // n_ens, features), BF16),
        pltpu.VMEM((per_block, out_block, features), BF16),
        pltpu.VMEM((n_sp, out_block, features), BF16),
        pltpu.VMEM((out_block, features), BF16),
        pltpu.VMEM((out_block, features), BF16),
        pltpu.VMEM(rows_blocks, BF16),
        pltpu.VMEM(rows_blocks, BF16),
        pltpu.SemaphoreType.DMA((8,)),
        pltpu.SemaphoreType.DMA((8,)),
        pltpu.SemaphoreType.DMA((8,)),
    ]
    mesh_grad, weight_grad = pl.pallas_call(
        functools.partial(kernel, n_ens, n_sp, 1.0 / math.sqrt(total)),
        out_shape=(
            jax.ShapeDtypeStruct((local_rows, features), F32),
            jax.ShapeDtypeStruct((out_block, features), F32),
        ),
        in_specs=[hbm] * 8 + [vmem] * 4,
        out_specs=(vmem, vmem),
        scratch_shapes=scratch,
        compiler_params=pltpu.CompilerParams(
            collective_id=0, has_side_effects=True, vmem_limit_bytes=60 * 1024 * 1024
        ),
    )(
        mesh_latent[0],
        grid_embed,
        w_send,
        w_recv,
        w_msg,
        w_node,
        w_out.T,
        target.T,
        jnp.pad(var_weight, (0, LANES - variables)).reshape(1, LANES),
        jnp.swapaxes(send_rows[0], 0, 1),
        edge_slot.T,
        edge_count.reshape(1, points),
    )
    return (mesh_grad[None], weight_grad)


def solution(mesh):
    in_specs = (
        P("ens", "space", None),
        P("space", None),
        P(),
        P(),
        P(),
        P(),
        P(),
        P("space", None),
        P(),
        P("space", None, None),
        P("space", None),
        P("space"),
    )
    out_specs = (P("ens", "space", None), P("space", None))
    return jax.shard_map(
        functools.partial(body, mesh.shape["ens"], mesh.shape["space"]),
        mesh=mesh,
        in_specs=in_specs,
        out_specs=out_specs,
        check_vma=False,
    )
```

time: 386 us -> 70.5 us (0.18)
  the two profiles are of different devices: /device:TPU:1 before, /device:TPU:9 now
where the time goes in v1:
time: 70.5 us; the launch traced here: 70.2 us
  Pallas kernels  66.1 us (94%)
  local copies, waits for them, and re-layouts  3.46 us (5%)
    pallas_call x1, Pallas kernels, body(): pl.pallas_call(functools.partial(kernel, n_ens, n_sp, 1.0 / math.sqrt(tot...  66.1 us
    unnamed x6, local copies, waits for them, and re-layouts  2.94 us

profile of v1, /device:TPU:9, one launch (start us, length us, event | category | flops | bytes accessed | tf_op | source)
XLA Modules:
  0.0 70.2 jit_solution(4429283609477676262)
XLA Ops:
  0.6 0.0 copy-start.1
  0.6 0.6 copy-done.1
  1.3 0.5 pad_bitcast_fusion.var_ref
  1.8 66.1 %shard_map.131 = (f32[128,512]{1,0:T(8,128)}, f32[16,512]{1,0:T(8,128)}) custom-call(bf16[128,512]{1,0:T(8,128)(2,1)} %bitcast.13, bf16[512,512]{1,0:T(8,128)(2,1)} %emb_h.1, bf16[512,512]{1,0:T(8,128)(2,1)} %w_send_h.1, bf16[512,512]{1,0:T(8,128)(2,1)} %w_recv_h.1, bf16[512,512]{1,0:T(8,128)(2,1)} %w_msg_h.1, bf16[512,512]{1,0:T(8,128)(2,1)} %w_node_h.1, ...), custom_call_target="tpu_custom_call" | custom-call | tf_op jit(solution)/shard_map/pallas_call | solution.py:523
  67.9 0.0 copy-start
  68.0 1.7 %copy.16 = f32[1,128,512]{2,1,0:T(8,128)} copy(f32[1,128,512]{2,1,0:T(8,128)} %bitcast.11) | data formatting | bytes 524288
  69.6 0.0 copy-done
  69.6 0.6 copy.17
Async XLA Ops:
  0.6 0.7 copy-start.1
  67.9 1.7 %copy-start = (f32[16,512]{1,0:T(8,128)S(1)}, f32[16,512]{1,0:T(8,128)}, u32[]{:S(2)}) copy-start(f32[16,512]{1,0:T(8,128)} %get-tuple-element.9) | copy-start | bytes 98308

commit v2 on v1

v2 whole, which is shorter than its diff:
```python
import functools
import math

import jax
import jax.numpy as jnp
from jax import lax
from jax.experimental import pallas as pl
from jax.experimental.pallas import tpu as pltpu
from jax.sharding import PartitionSpec as P

MESH = pl.DeviceIdType.MESH
F32 = jnp.float32
BF16 = jnp.bfloat16
SOFT = 0.09
LANES = 128
ALONG_X = 4
PARTS = 2


def sigmoid(v):
    return 0.5 * jnp.tanh(0.5 * v) + 0.5


def dot(a, b):
    return jnp.dot(a, b, preferred_element_type=F32)


def dot_t(a, b):
    return lax.dot_general(a, b, (((1,), (1,)), ((), ())), preferred_element_type=F32)


def to_blocks(rows, n):
    c, f = rows.shape[0] // n, rows.shape[1]
    split = rows.reshape(n, c, f)
    return jnp.concatenate([split[:, :, : f // 2], split[:, :, f // 2 :]], axis=1)


def from_blocks(blocks):
    n, c2, f2 = blocks.shape
    c = c2 // 2
    left = blocks[:, :c, :].reshape(n * c, f2)
    right = blocks[:, c:, :].reshape(n * c, f2)
    return jnp.concatenate([left, right], axis=1)


def wrap(i, n):
    return jnp.where(i < 0, i + n, jnp.where(i >= n, i - n, i))


def from_far(t, n):
    return n // 2 + (1 - 2 * lax.rem(t, 2)) * lax.div(t + 1, 2)


def kernel(
    n_ens,
    n_sp,
    scale,
    lat_h,
    emb_h,
    w_send_h,
    w_recv_h,
    w_msg_h,
    w_node_h,
    w_out_h,
    target_h,
    var_h,
    rows_h,
    slot_h,
    count_h,
    rows_grad_ref,
    w_send_ref,
    weight_ref,
    lat,
    rows_ref,
    emb,
    w_recv,
    w_msg,
    w_node,
    w_out_raw,
    target_raw,
    var_ref,
    slot_ref,
    count_ref,
    wide,
    w_out,
    target_wide,
    target,
    var_wide,
    small,
    columns,
    pick,
    pick_t,
    out_rows,
    in_rows,
    slot_proj,
    grid_proj,
    one_hot,
    one_hot_t,
    pre,
    live,
    summed_act,
    summed_act_t,
    node_pre,
    pred,
    pred_in,
    grad_wide,
    grad_out,
    grad_in,
    pred_grad,
    edge_grad,
    back,
    pre_grad,
    slot_grad,
    halves,
    pair_out,
    pair_in,
    sum_out,
    sum_in,
    total_out,
    total_in,
    rows_out,
    rows_in,
    load_sem,
    send_sem,
    recv_sem,
):
    ens = lax.axis_index("ens")
    sp = lax.axis_index("space")
    core = lax.rem(ens, 2)
    n_x = ALONG_X
    n_y = n_sp // n_x
    y = lax.div(sp, n_x)
    x = lax.rem(sp, n_x)
    points, features = emb.shape
    per_point = slot_ref.shape[0]
    cap = rows_ref.shape[0]
    slots = n_sp * cap
    part_points = points // PARTS
    half = features // 2
    w_send = w_send_ref

    loads = [
        pltpu.make_async_copy(src, dst, load_sem.at[i])
        for i, (src, dst) in enumerate(
            [
                (rows_h, rows_ref),
                (lat_h, lat),
                (emb_h, emb),
                (w_recv_h, w_recv),
                (slot_h, slot_ref),
                (count_h, count_ref),
                (w_send_h, w_send),
                (w_msg_h, w_msg),
                (w_node_h, w_node),
                (w_out_h, w_out_raw),
                (target_h, target_raw),
                (var_h, var_ref),
            ]
        )
    ]
    for load in loads:
        load.start()

    def space_peer(t):
        dy = from_far(lax.div(t, n_x), n_y)
        dx = from_far(lax.rem(t, n_x), n_x)
        to = lax.rem(y + dy, n_y) * n_x + lax.rem(x + dx, n_x)
        back_place = lax.rem(n_y - dy, n_y) * n_x + lax.rem(n_x - dx, n_x)
        return to, dy * n_x + dx, back_place

    barrier = pltpu.get_barrier_semaphore()

    @pl.loop(0, n_sp - 1)
    def _(t):
        to, _, _ = space_peer(t)
        pl.semaphore_signal(barrier, inc=1, device_id={"space": to}, device_id_type=MESH)

    @pl.loop(0, n_ens - 1)
    def _(t):
        to = lax.rem(ens + from_far(t, n_ens), n_ens)
        pl.semaphore_signal(barrier, inc=1, device_id={"ens": to}, device_id_type=MESH)

    def remote(src, dst, which, to):
        return pltpu.make_async_remote_copy(
            src_ref=src,
            dst_ref=dst,
            send_sem=send_sem.at[which],
            recv_sem=recv_sem.at[which],
            device_id=to,
            device_id_type=MESH,
        )

    def whole(ref, which):
        return remote(ref, ref, which, {"ens": ens})

    loads[0].wait()
    tiled = jnp.broadcast_to(
        rows_ref[...].astype(F32)[None], (n_sp, cap, n_sp)
    ).reshape(slots, n_sp)
    place = lax.broadcasted_iota(jnp.int32, (slots, n_sp), 0) // cap
    receiver = wrap(place // n_x + y, n_y) * n_x + wrap(place % n_x + x, n_x)
    lane = lax.broadcasted_iota(jnp.int32, (slots, n_sp), 1)
    wanted = jnp.sum(jnp.where(lane == receiver, tiled, 0.0), axis=1, keepdims=True)
    local_rows = lat.shape[0]
    pick_wide = jnp.where(
        lax.broadcasted_iota(jnp.int32, (slots, local_rows), 1).astype(F32) == wanted, 1.0, 0.0
    )
    pick[...] = pick_wide.astype(BF16)
    loads[1].wait()
    blocks = to_blocks(dot(pick[...], lat[...]), n_sp).astype(BF16)
    out_rows[...] = blocks
    in_rows[0] = blocks[0]
    pl.semaphore_wait(barrier, n_sp + n_ens - 2)

    def space_exchange(src, dst, which):
        @pl.loop(0, n_sp - 1)
        def _(t):
            to, place, back_place = space_peer(t)
            remote(src.at[place], dst.at[back_place], which, {"space": to}).start()

    space_exchange(out_rows, in_rows, 0)

    loads[2].wait()
    loads[3].wait()
    grid_proj[...] = dot(emb[...], w_recv[...])
    pick_t[...] = jnp.transpose(pick_wide).astype(BF16)
    loads[4].wait()
    loads[5].wait()
    sender = slot_ref[...] // cap
    slot = (
        wrap(sender // n_x - y, n_y) * n_x + wrap(sender % n_x - x, n_x)
    ) * cap + slot_ref[...] % cap
    is_live = lax.broadcasted_iota(jnp.int32, slot.shape, 0) < count_ref[...]
    small[...] = jnp.zeros_like(small)
    small[0:per_point, :] = slot.astype(F32)
    small[per_point : 2 * per_point, :] = jnp.where(is_live, 1.0, 0.0)
    columns[...] = jnp.transpose(small[...])
    slot = jnp.where(is_live, slot, -1)
    slot_index = lax.broadcasted_iota(jnp.int32, (slots, part_points), 0)
    lane_index = lax.broadcasted_iota(jnp.int32, (points, slots), 1).astype(F32)
    for k in range(per_point):
        one_hot[k] = jnp.where(lane_index == columns[:, k : k + 1], 1.0, 0.0).astype(BF16)
        for h in range(PARTS):
            one_hot_t[h, :, k * part_points : (k + 1) * part_points] = jnp.where(
                slot_index == slot[k : k + 1, h * part_points : (h + 1) * part_points], 1.0, 0.0
            ).astype(BF16)
        live[k] = jnp.broadcast_to(
            columns[:, per_point + k : per_point + k + 1], (points, LANES)
        )
    loads[9].wait()
    variables = w_out_raw.shape[0]
    wide[...] = jnp.zeros_like(wide)
    wide[0:variables, :] = w_out_raw[...].astype(F32)
    w_out[...] = wide[...].astype(BF16)
    loads[10].wait()
    target_wide[...] = jnp.zeros_like(target_wide)
    target_wide[0:variables, :] = target_raw[...]
    target[...] = jnp.transpose(target_wide[...])
    loads[11].wait()
    var_wide[...] = jnp.zeros_like(var_wide)
    var_wide[0:1, 0:variables] = var_ref[...]
    loads[6].wait()
    loads[7].wait()
    loads[8].wait()

    step = 16

    def rows_of(h, i):
        return pl.ds(pl.multiple_of(h * part_points + i * step, step), step)

    def spread(k, rows):
        return jnp.concatenate([live[k, rows, :]] * (features // LANES), axis=1)

    def forward(h):
        span = pl.ds(h * part_points, part_points)
        for k in range(per_point):
            pre[k, span, :] = dot(one_hot[k, span, :], slot_proj[...])

        @pl.loop(0, part_points // step)
        def _(i):
            rows = rows_of(h, i)
            base = grid_proj[rows, :]
            total = jnp.zeros((step, features), F32)
            for k in range(per_point):
                v = pre[k, rows, :] + base
                total += v * sigmoid(v) * spread(k, rows)
            summed_act[rows, :] = total.astype(BF16)

        node_in = (
            dot(summed_act[span, :], w_msg[...]) + emb[span, :].astype(F32)
        ).astype(BF16)
        v = dot(node_in, w_node[...])
        node_pre[span, :] = v
        hidden = (v * sigmoid(v)).astype(BF16)
        pred[h] = dot_t(hidden, w_out[...]).reshape(pred.shape[1:])

        pred_in[h, 0] = pred[h, ens]

        @pl.loop(0, n_ens - 1)
        def _(t):
            q = from_far(t, n_ens)
            to = lax.rem(ens + q, n_ens)
            remote(pred.at[h, to], pred_in.at[h, n_ens - q], 1 + h, {"ens": to}).start()

    def slopes(h):
        @pl.loop(0, part_points // step)
        def _(i):
            rows = rows_of(h, i)
            base = grid_proj[rows, :]
            for k in range(per_point):
                v = pre[k, rows, :] + base
                s = sigmoid(v)
                pre[k, rows, :] = s * (1.0 + v * (1.0 - s))
            v = node_pre[rows, :]
            s = sigmoid(v)
            node_pre[rows, :] = s * (1.0 + v * (1.0 - s))

    def scores(h):
        whole(pred_in.at[h, pl.ds(1, n_ens - 1)], 1 + h).wait_recv()
        share = part_points // n_ens

        @pl.loop(0, share // 8)
        def _(i):
            rows = pl.ds(pl.multiple_of(i * 8, 8), 8)
            goal = target[
                pl.ds(pl.multiple_of(h * part_points + ens * share + i * 8, 8), 8), :
            ]
            mine = [pred_in[h, m, rows, :] for m in range(n_ens)]
            pairwise = [jnp.zeros_like(goal) for _ in range(n_ens)]
            for a in range(n_ens):
                for b in range(a + 1, n_ens):
                    t = mine[a] - mine[b]
                    g = t * lax.rsqrt(t * t + SOFT)
                    pairwise[a] += g
                    pairwise[b] -= g
            weight_row = var_wide[0:1, :]
            for m in range(n_ens):
                t = mine[m] - goal
                g = t * lax.rsqrt(t * t + SOFT)
                grad_wide[m, rows, :] = weight_row * (g - pairwise[m] * (1.0 / (n_ens - 1.0)))

        grad_out[h] = grad_wide[...].astype(BF16)
        grad_in[h, 0] = grad_out[h, 0]

        @pl.loop(0, n_ens - 1)
        def _(t):
            q = from_far(t, n_ens)
            to = lax.rem(ens + q, n_ens)
            remote(
                grad_out.at[h, q], grad_in.at[h, n_ens - q], 1 + PARTS + h, {"ens": to}
            ).start()

    def edge_backward(h):
        whole(grad_in.at[h, pl.ds(1, n_ens - 1)], 1 + PARTS + h).wait_recv()

        @pl.loop(0, n_ens)
        def _(q):
            pred_grad[h, lax.rem(ens + q, n_ens)] = grad_in[h, q]

        span = pl.ds(h * part_points, part_points)
        hidden_grad = (
            dot(pred_grad[h].reshape(part_points, LANES), w_out[...]) * node_pre[span, :]
        ).astype(BF16)
        edge_grad[h] = dot_t(hidden_grad, w_node[...]).astype(BF16)

    def weight_half(which, h):
        return dot(summed_act_t[which, :, h * part_points : (h + 1) * part_points], edge_grad[h])

    def slot_backward(h):
        @pl.loop(0, part_points // step)
        def _(i):
            rows = rows_of(h, i)
            b = back[pl.ds(pl.multiple_of(i * step, step), step), :]
            for k in range(per_point):
                pre_grad[
                    pl.ds(pl.multiple_of(k * part_points + i * step, step), step), :
                ] = (b * pre[k, rows, :]).astype(BF16)

        return dot(one_hot_t[h], pre_grad[...])

    whole(in_rows.at[pl.ds(1, n_sp - 1)], 0).wait_recv()
    arrived = from_blocks(in_rows[...].astype(F32)).astype(BF16)
    slot_proj[...] = dot(arrived, w_send[...]).astype(BF16)
    for h in range(PARTS):
        forward(h)

    for h in range(PARTS):
        slopes(h)
    turned = jnp.transpose(summed_act[...].astype(F32)).reshape(n_sp, 2, features // n_sp // 2, points)
    for c in range(2):
        summed_act_t[c] = turned[:, c].reshape(half, points).astype(BF16)

    for h in range(PARTS):
        scores(h)

    theirs, ours = 1 - core, core
    for h in range(PARTS - 1):
        edge_backward(h)
        back[...] = dot_t(edge_grad[h], w_msg[...])
        for i, which in enumerate((theirs, ours)):
            term = weight_half(which, h)
            halves[i] = term if h == 0 else halves[i] + term
        term = slot_backward(h)
        slot_grad[...] = term if h == 0 else slot_grad[...] + term

    last = PARTS - 1
    edge_backward(last)
    pair_out[...] = (halves[0] + weight_half(theirs, last)).astype(BF16)
    pair = remote(pair_out, pair_in, 7, {"ens": ens + 1 - 2 * core})
    pair.start()
    back[...] = dot_t(edge_grad[last], w_msg[...])
    own = halves[1] + weight_half(ours, last)
    halves[1] = own
    pair.wait_recv()
    blocks = to_blocks(halves[1] + pair_in[...].astype(F32), n_sp).astype(BF16)
    sum_out[...] = blocks
    sum_in[0] = sum_out[sp]

    @pl.loop(0, n_sp - 1)
    def _(t):
        to, _, back_place = space_peer(t)
        remote(sum_out.at[to], sum_in.at[back_place], 5, {"space": to}).start()

    blocks = to_blocks(slot_grad[...] + slot_backward(last), n_sp).astype(BF16)
    rows_out[...] = blocks
    rows_in[0] = blocks[0]
    space_exchange(rows_out, rows_in, 6)

    whole(sum_in.at[pl.ds(1, n_sp - 1)], 5).wait_recv()
    total_out[...] = jnp.sum(sum_in[...].astype(F32), axis=0).astype(BF16)
    total_in[0] = total_out[...]

    @pl.loop(0, n_ens - 1)
    def _(t):
        q = from_far(t, n_ens)
        to = lax.rem(ens + q, n_ens)
        remote(total_out, total_in.at[n_ens - q], 8, {"ens": to}).start()

    whole(rows_in.at[pl.ds(1, n_sp - 1)], 6).wait_recv()
    back_rows = from_blocks(rows_in[...].astype(F32)).astype(BF16)
    rows_grad_ref[...] = dot(pick_t[...], back_rows)

    whole(total_in.at[pl.ds(1, n_ens - 1)], 8).wait_recv()
    same = total_in[0].astype(F32)
    other = total_in[1].astype(F32)
    for q in range(2, n_ens, 2):
        same += total_in[q].astype(F32)
        other += total_in[q + 1].astype(F32)
    first = jnp.where(core == 0, same, other)
    second = jnp.where(core == 0, other, same)
    weight_ref[...] = scale * jnp.concatenate(
        [from_blocks(first[None]), from_blocks(second[None])], axis=0
    )

    whole(out_rows.at[pl.ds(1, n_sp - 1)], 0).wait_send()
    for h in range(PARTS):
        whole(pred_in.at[h, pl.ds(1, n_ens - 1)], 1 + h).wait_send()
        whole(grad_out.at[h, pl.ds(1, n_ens - 1)], 1 + PARTS + h).wait_send()
    pair.wait_send()
    whole(sum_in.at[pl.ds(1, n_sp - 1)], 5).wait_send()
    whole(rows_out.at[pl.ds(1, n_sp - 1)], 6).wait_send()
    whole(total_in.at[pl.ds(1, n_ens - 1)], 8).wait_send()


def last_kernel(rows_ref, w_send_ref, weight_in, mesh_ref, weight_ref):
    rows = rows_ref[...]
    high = rows.astype(BF16)
    low = (rows - high.astype(F32)).astype(BF16)
    mesh_ref[...] = dot_t(high, w_send_ref[...]) + dot_t(low, w_send_ref[...])
    weight_ref[...] = weight_in[...]


def body(
    n_ens,
    n_sp,
    mesh_latent,
    grid_embed,
    w_send,
    w_recv,
    w_msg,
    w_node,
    w_out,
    target,
    var_weight,
    send_rows,
    edge_slot,
    edge_count,
):
    local_rows, features = mesh_latent.shape[1:]
    points, per_point = edge_slot.shape
    variables = target.shape[1]
    cap = send_rows.shape[2]
    slots = n_sp * cap
    part_points = points // PARTS
    share = part_points // n_ens
    half = features // 2
    out_block = features // n_sp
    total = n_ens * points * n_sp * per_point
    hbm = pl.BlockSpec(memory_space=pltpu.HBM)
    vmem = pl.BlockSpec(memory_space=pltpu.VMEM)
    square = (features, features)
    rows_blocks = (n_sp, 2 * cap, half)
    shares = (PARTS, n_ens, share, LANES)
    scratch = [
        pltpu.VMEM((local_rows, features), BF16),
        pltpu.VMEM((cap, n_sp), jnp.int32),
        pltpu.VMEM((points, features), BF16),
        pltpu.VMEM(square, BF16),
        pltpu.VMEM(square, BF16),
        pltpu.VMEM(square, BF16),
        pltpu.VMEM((variables, features), BF16),
        pltpu.VMEM((variables, points), F32),
        pltpu.VMEM((1, variables), F32),
        pltpu.VMEM((per_point, points), jnp.int32),
        pltpu.VMEM((1, points), jnp.int32),
        pltpu.VMEM((LANES, features), F32),
        pltpu.VMEM((LANES, features), BF16),
        pltpu.VMEM((LANES, points), F32),
        pltpu.VMEM((points, LANES), F32),
        pltpu.VMEM((8, LANES), F32),
        pltpu.VMEM((LANES, points), F32),
        pltpu.VMEM((points, LANES), F32),
        pltpu.VMEM((slots, local_rows), BF16),
        pltpu.VMEM((local_rows, slots), BF16),
        pltpu.VMEM(rows_blocks, BF16),
        pltpu.VMEM(rows_blocks, BF16),
        pltpu.VMEM((slots, features), BF16),
        pltpu.VMEM((points, features), F32),
        pltpu.VMEM((per_point, points, slots), BF16),
        pltpu.VMEM((PARTS, slots, per_point * part_points), BF16),
        pltpu.VMEM((per_point, points, features), F32),
        pltpu.VMEM((per_point, points, LANES), F32),
        pltpu.VMEM((points, features), BF16),
        pltpu.VMEM((2, half, points), BF16),
        pltpu.VMEM((points, features), F32),
        pltpu.VMEM(shares, F32),
        pltpu.VMEM(shares, F32),
        pltpu.VMEM(shares[1:], F32),
        pltpu.VMEM(shares, BF16),
        pltpu.VMEM(shares, BF16),
        pltpu.VMEM(shares, BF16),
        pltpu.VMEM((PARTS, part_points, features), BF16),
        pltpu.VMEM((part_points, features), F32),
        pltpu.VMEM((per_point * part_points, features), BF16),
        pltpu.VMEM((slots, features), F32),
        pltpu.VMEM((2, half, features), F32),
        pltpu.VMEM((half, features), BF16),
        pltpu.VMEM((half, features), BF16),
        pltpu.VMEM((n_sp, out_block, half), BF16),
        pltpu.VMEM((n_sp, out_block, half), BF16),
        pltpu.VMEM((out_block, half), BF16),
        pltpu.VMEM((n_ens, out_block, half), BF16),
        pltpu.VMEM(rows_blocks, BF16),
        pltpu.VMEM(rows_blocks, BF16),
        pltpu.SemaphoreType.DMA((12,)),
        pltpu.SemaphoreType.DMA((9,)),
        pltpu.SemaphoreType.DMA((9,)),
    ]
    row_grads, w_send_near, weight_grad = pl.pallas_call(
        functools.partial(kernel, n_ens, n_sp, 1.0 / math.sqrt(total)),
        out_shape=(
            jax.ShapeDtypeStruct((local_rows, features), F32),
            jax.ShapeDtypeStruct(square, BF16),
            jax.ShapeDtypeStruct((out_block, features), F32),
        ),
        in_specs=[hbm] * 12,
        out_specs=(vmem, vmem, vmem),
        scratch_shapes=scratch,
        compiler_params=pltpu.CompilerParams(
            collective_id=0, has_side_effects=True, vmem_limit_bytes=48 * 1024 * 1024
        ),
    )(
        *(
            pltpu.with_memory_space_constraint(array, pltpu.HBM)
            for array in (
                mesh_latent[0],
                grid_embed,
                w_send,
                w_recv,
                w_msg,
                w_node,
                w_out.T,
                target.T,
                var_weight.reshape(1, variables),
                jnp.swapaxes(send_rows[0], 0, 1),
                edge_slot.T,
                edge_count.reshape(1, points),
            )
        )
    )
    mesh_grad, weight_grad = pl.pallas_call(
        last_kernel,
        out_shape=(
            jax.ShapeDtypeStruct((local_rows, features), F32),
            jax.ShapeDtypeStruct((out_block, features), F32),
        ),
        in_specs=[vmem] * 3,
        out_specs=(vmem, vmem),
    )(row_grads, w_send_near, weight_grad)
    return (mesh_grad[None], weight_grad)


def solution(mesh):
    in_specs = (
        P("ens", "space", None),
        P("space", None),
        P(),
        P(),
        P(),
        P(),
        P(),
        P("space", None),
        P(),
        P("space", None, None),
        P("space", None),
        P("space"),
    )
    out_specs = (P("ens", "space", None), P("space", None))
    return jax.shard_map(
        functools.partial(body, mesh.shape["ens"], mesh.shape["space"]),
        mesh=mesh,
        in_specs=in_specs,
        out_specs=out_specs,
        check_vma=False,
    )
```

time: 70.5 us -> 62.8 us (0.89)
  the two profiles are of different devices: /device:TPU:9 before, /device:TPU:1 now
where the time goes in v2:
time: 62.8 us; the launch traced here: 62.7 us
  Pallas kernels  59.9 us (95%)
  local copies, waits for them, and re-layouts  2.09 us (3%)
  between operations  0.65 us (1%)
    pallas_call x1, Pallas kernels, body(): pl.pallas_call(functools.partial(kernel, n_ens, n_sp, 1.0 / math.sqrt(tot...  57.7 us
    pallas_call x1, Pallas kernels, body(): pl.pallas_call(last_kernel, out_shape=(jax.ShapeDtypeStruct((local_rows,...  2.29 us
    unnamed x6, local copies, waits for them, and re-layouts  2.09 us

profile of v2, /device:TPU:1, one launch (start us, length us, event | category | flops | bytes accessed | tf_op | source)
XLA Modules:
  0.0 62.7 jit_solution(10170345473999431884)
XLA Ops:
  0.6 57.7 %shard_map.131 = (f32[128,512]{1,0:T(8,128)S(1)}, bf16[512,512]{1,0:T(8,128)(2,1)S(1)}, f32[16,512]{1,0:T(8,128)S(1)}) custom-call(bf16[128,512]{1,0:T(8,128)(2,1)} %bitcast.11, bf16[512,512]{1,0:T(8,128)(2,1)} %emb_h.1, bf16[512,512]{1,0:T(8,128)(2,1)} %w_send_h.1, bf16[512,512]{1,0:T(8,128)(2,1)} %w_recv_h.1, bf16[512,512]{1,0:T(8,128)(2,1)} %w_msg_h.1, ...), custom_call_target="tpu_custom_call" | custom-call | tf_op jit(solution)/shard_map/pallas_call | solution.py:559
  58.3 0.0 copy-start
  58.3 0.8 %copy-done = bf16[512,512]{1,0:T(8,128)(2,1)} copy-done((bf16[512,512]{1,0:T(8,128)(2,1)}, bf16[512,512]{1,0:T(8,128)(2,1)S(1)}, u32[]{:S(2)}) %copy-start) | copy-done | bytes 524312
  59.1 0.0 copy-start.1
  59.1 0.7 %copy-done.1 = f32[128,512]{1,0:T(8,128)} copy-done((f32[128,512]{1,0:T(8,128)}, f32[128,512]{1,0:T(8,128)S(1)}, u32[]{:S(2)}) %copy-start.1) | copy-done | bytes 262168
  59.8 0.0 copy-start.2
  59.8 0.6 copy-done.2
  60.4 2.3 %shard_map.132 = (f32[128,512]{1,0:T(8,128)}, f32[16,512]{1,0:T(8,128)}) custom-call(f32[128,512]{1,0:T(8,128)} %copy-done.1, bf16[512,512]{1,0:T(8,128)(2,1)} %copy-done, f32[16,512]{1,0:T(8,128)} %copy-done.2), custom_call_target="tpu_custom_call" | custom-call | tf_op jit(solution)/shard_map/pallas_call | solution.py:591
Async XLA Ops:
  58.3 0.8 %copy-start = (bf16[512,512]{1,0:T(8,128)(2,1)}, bf16[512,512]{1,0:T(8,128)(2,1)S(1)}, u32[]{:S(2)}) copy-start(bf16[512,512]{1,0:T(8,128)(2,1)S(1)} %get-tuple-element.8.w_send_ref) | copy-start | bytes 1572868
  59.1 0.7 %copy-start.1 = (f32[128,512]{1,0:T(8,128)}, f32[128,512]{1,0:T(8,128)S(1)}, u32[]{:S(2)}) copy-start(f32[128,512]{1,0:T(8,128)S(1)} %get-tuple-element.7.rows_ref) | copy-start | bytes 786436
  59.8 0.6 copy-start.2

commit v3 on v2

--- a/solution.py
+++ b/solution.py
@@ -17,8 +17,13 @@
 PARTS = 2
 
 
-def sigmoid(v):
-    return 0.5 * jnp.tanh(0.5 * v) + 0.5
+def silu(u):
+    return u * jnp.tanh(u) + u
+
+
+def twice_slope(u):
+    t = jnp.tanh(u)
+    return 1.0 + t + u * (1.0 - t * t)
 
 
 def dot(a, b):
@@ -67,12 +72,12 @@
     rows_h,
     slot_h,
     count_h,
-    rows_grad_ref,
-    w_send_ref,
+    mesh_ref,
     weight_ref,
     lat,
     rows_ref,
     emb,
+    w_send,
     w_recv,
     w_msg,
     w_node,
@@ -103,6 +108,7 @@
     node_pre,
     pred,
     pred_in,
+    pred_wide,
     grad_wide,
     grad_out,
     grad_in,
@@ -137,7 +143,25 @@
     slots = n_sp * cap
     part_points = points // PARTS
     half = features // 2
-    w_send = w_send_ref
+
+    def space_peer(t):
+        dy = from_far(lax.div(t, n_x), n_y)
+        dx = from_far(lax.rem(t, n_x), n_x)
+        to = lax.rem(y + dy, n_y) * n_x + lax.rem(x + dx, n_x)
+        back_place = lax.rem(n_y - dy, n_y) * n_x + lax.rem(n_x - dx, n_x)
+        return to, dy * n_x + dx, back_place
+
+    barrier = pltpu.get_barrier_semaphore()
+
+    @pl.loop(0, n_sp - 1)
+    def _(t):
+        to, _, _ = space_peer(t)
+        pl.semaphore_signal(barrier, inc=1, device_id={"space": to}, device_id_type=MESH)
+
+    @pl.loop(0, n_ens - 1)
+    def _(t):
+        to = lax.rem(ens + from_far(t, n_ens), n_ens)
+        pl.semaphore_signal(barrier, inc=1, device_id={"ens": to}, device_id_type=MESH)
 
     loads = [
         pltpu.make_async_copy(src, dst, load_sem.at[i])
@@ -161,25 +185,6 @@
     for load in loads:
         load.start()
 
-    def space_peer(t):
-        dy = from_far(lax.div(t, n_x), n_y)
-        dx = from_far(lax.rem(t, n_x), n_x)
-        to = lax.rem(y + dy, n_y) * n_x + lax.rem(x + dx, n_x)
-        back_place = lax.rem(n_y - dy, n_y) * n_x + lax.rem(n_x - dx, n_x)
-        return to, dy * n_x + dx, back_place
-
-    barrier = pltpu.get_barrier_semaphore()
-
-    @pl.loop(0, n_sp - 1)
-    def _(t):
-        to, _, _ = space_peer(t)
-        pl.semaphore_signal(barrier, inc=1, device_id={"space": to}, device_id_type=MESH)
-
-    @pl.loop(0, n_ens - 1)
-    def _(t):
-        to = lax.rem(ens + from_far(t, n_ens), n_ens)
-        pl.semaphore_signal(barrier, inc=1, device_id={"ens": to}, device_id_type=MESH)
-
     def remote(src, dst, which, to):
         return pltpu.make_async_remote_copy(
             src_ref=src,
@@ -222,7 +227,7 @@
 
     loads[2].wait()
     loads[3].wait()
-    grid_proj[...] = dot(emb[...], w_recv[...])
+    grid_proj[...] = 0.5 * dot(emb[...], w_recv[...])
     pick_t[...] = jnp.transpose(pick_wide).astype(BF16)
     loads[4].wait()
     loads[5].wait()
@@ -273,26 +278,26 @@
 
     def forward(h):
         span = pl.ds(h * part_points, part_points)
-        for k in range(per_point):
-            pre[k, span, :] = dot(one_hot[k, span, :], slot_proj[...])
-
-        @pl.loop(0, part_points // step)
-        def _(i):
-            rows = rows_of(h, i)
-            base = grid_proj[rows, :]
-            total = jnp.zeros((step, features), F32)
-            for k in range(per_point):
-                v = pre[k, rows, :] + base
-                total += v * sigmoid(v) * spread(k, rows)
-            summed_act[rows, :] = total.astype(BF16)
+        for m in range(0, part_points, 128):
+            rows = pl.ds(h * part_points + m, 128)
+            for n in range(0, features, 256):
+                lanes = pl.ds(n, 256)
+                base = grid_proj[rows, lanes]
+                total = jnp.zeros((128, 256), F32)
+                for k in range(per_point):
+                    u = dot(one_hot[k, rows, :], slot_proj[:, lanes]) + base
+                    pre[k, rows, lanes] = u
+                    mask = jnp.concatenate([live[k, rows, :]] * 2, axis=1)
+                    total += silu(u) * mask
+                summed_act[rows, lanes] = total.astype(BF16)
 
         node_in = (
             dot(summed_act[span, :], w_msg[...]) + emb[span, :].astype(F32)
         ).astype(BF16)
-        v = dot(node_in, w_node[...])
-        node_pre[span, :] = v
-        hidden = (v * sigmoid(v)).astype(BF16)
-        pred[h] = dot_t(hidden, w_out[...]).reshape(pred.shape[1:])
+        u = 0.5 * dot(node_in, w_node[...])
+        node_pre[span, :] = u
+        hidden = silu(u).astype(BF16)
+        pred[h] = dot_t(hidden, w_out[...]).reshape(pred.shape[1:]).astype(BF16)
 
         pred_in[h, 0] = pred[h, ens]
 
@@ -308,15 +313,12 @@
             rows = rows_of(h, i)
             base = grid_proj[rows, :]
             for k in range(per_point):
-                v = pre[k, rows, :] + base
-                s = sigmoid(v)
-                pre[k, rows, :] = s * (1.0 + v * (1.0 - s))
-            v = node_pre[rows, :]
-            s = sigmoid(v)
-            node_pre[rows, :] = s * (1.0 + v * (1.0 - s))
+                pre[k, rows, :] = twice_slope(pre[k, rows, :])
+            node_pre[rows, :] = 0.5 * twice_slope(node_pre[rows, :])
 
     def scores(h):
         whole(pred_in.at[h, pl.ds(1, n_ens - 1)], 1 + h).wait_recv()
+        pred_wide[...] = pred_in[h].astype(F32)
         share = part_points // n_ens
 
         @pl.loop(0, share // 8)
@@ -325,7 +327,7 @@
             goal = target[
                 pl.ds(pl.multiple_of(h * part_points + ens * share + i * 8, 8), 8), :
             ]
-            mine = [pred_in[h, m, rows, :] for m in range(n_ens)]
+            mine = [pred_wide[m, rows, :] for m in range(n_ens)]
             pairwise = [jnp.zeros_like(goal) for _ in range(n_ens)]
             for a in range(n_ens):
                 for b in range(a + 1, n_ens):
@@ -370,17 +372,15 @@
         @pl.loop(0, part_points // step)
         def _(i):
             rows = rows_of(h, i)
-            b = back[pl.ds(pl.multiple_of(i * step, step), step), :]
+            b = 0.5 * back[pl.ds(pl.multiple_of(i * step, step), step), :]
             for k in range(per_point):
                 pre_grad[
                     pl.ds(pl.multiple_of(k * part_points + i * step, step), step), :
                 ] = (b * pre[k, rows, :]).astype(BF16)
 
-        return dot(one_hot_t[h], pre_grad[...])
-
     whole(in_rows.at[pl.ds(1, n_sp - 1)], 0).wait_recv()
     arrived = from_blocks(in_rows[...].astype(F32)).astype(BF16)
-    slot_proj[...] = dot(arrived, w_send[...]).astype(BF16)
+    slot_proj[...] = (0.5 * dot(arrived, w_send[...])).astype(BF16)
     for h in range(PARTS):
         forward(h)
 
@@ -400,7 +400,8 @@
         for i, which in enumerate((theirs, ours)):
             term = weight_half(which, h)
             halves[i] = term if h == 0 else halves[i] + term
-        term = slot_backward(h)
+        slot_backward(h)
+        term = dot(one_hot_t[h], pre_grad[...])
         slot_grad[...] = term if h == 0 else slot_grad[...] + term
 
     last = PARTS - 1
@@ -411,6 +412,7 @@
     back[...] = dot_t(edge_grad[last], w_msg[...])
     own = halves[1] + weight_half(ours, last)
     halves[1] = own
+    slot_backward(last)
     pair.wait_recv()
     blocks = to_blocks(halves[1] + pair_in[...].astype(F32), n_sp).astype(BF16)
     sum_out[...] = blocks
@@ -421,7 +423,9 @@
         to, _, back_place = space_peer(t)
         remote(sum_out.at[to], sum_in.at[back_place], 5, {"space": to}).start()
 
-    blocks = to_blocks(slot_grad[...] + slot_backward(last), n_sp).astype(BF16)
+    blocks = to_blocks(
+        slot_grad[...] + dot(one_hot_t[last], pre_grad[...]), n_sp
+    ).astype(BF16)
     rows_out[...] = blocks
     rows_in[0] = blocks[0]
     space_exchange(rows_out, rows_in, 6)
@@ -438,7 +442,10 @@
 
     whole(rows_in.at[pl.ds(1, n_sp - 1)], 6).wait_recv()
     back_rows = from_blocks(rows_in[...].astype(F32)).astype(BF16)
-    rows_grad_ref[...] = dot(pick_t[...], back_rows)
+    row_grads = dot(pick_t[...], back_rows)
+    high = row_grads.astype(BF16)
+    low = (row_grads - high.astype(F32)).astype(BF16)
+    mesh_ref[...] = dot_t(high, w_send[...]) + dot_t(low, w_send[...])
 
     whole(total_in.at[pl.ds(1, n_ens - 1)], 8).wait_recv()
     same = total_in[0].astype(F32)
@@ -462,12 +469,15 @@
     whole(total_in.at[pl.ds(1, n_ens - 1)], 8).wait_send()
 
 
-def last_kernel(rows_ref, w_send_ref, weight_in, mesh_ref, weight_ref):
-    rows = rows_ref[...]
-    high = rows.astype(BF16)
-    low = (rows - high.astype(F32)).astype(BF16)
-    mesh_ref[...] = dot_t(high, w_send_ref[...]) + dot_t(low, w_send_ref[...])
-    weight_ref[...] = weight_in[...]
+def write_out(mesh_in, weight_in, mesh_ref, weight_ref, sem):
+    copies = [
+        pltpu.make_async_copy(mesh_in, mesh_ref, sem.at[0]),
+        pltpu.make_async_copy(weight_in, weight_ref, sem.at[1]),
+    ]
+    for copy in copies:
+        copy.start()
+    for copy in copies:
+        copy.wait()
 
 
 def body(
@@ -508,6 +518,7 @@
         pltpu.VMEM(square, BF16),
         pltpu.VMEM(square, BF16),
         pltpu.VMEM(square, BF16),
+        pltpu.VMEM(square, BF16),
         pltpu.VMEM((variables, features), BF16),
         pltpu.VMEM((variables, points), F32),
         pltpu.VMEM((1, variables), F32),
@@ -533,8 +544,9 @@
         pltpu.VMEM((points, features), BF16),
         pltpu.VMEM((2, half, points), BF16),
         pltpu.VMEM((points, features), F32),
-        pltpu.VMEM(shares, F32),
-        pltpu.VMEM(shares, F32),
+        pltpu.VMEM(shares, BF16),
+        pltpu.VMEM(shares, BF16),
+        pltpu.VMEM(shares[1:], F32),
         pltpu.VMEM(shares[1:], F32),
         pltpu.VMEM(shares, BF16),
         pltpu.VMEM(shares, BF16),
@@ -556,15 +568,14 @@
         pltpu.SemaphoreType.DMA((9,)),
         pltpu.SemaphoreType.DMA((9,)),
     ]
-    row_grads, w_send_near, weight_grad = pl.pallas_call(
+    mesh_grad, weight_grad = pl.pallas_call(
         functools.partial(kernel, n_ens, n_sp, 1.0 / math.sqrt(total)),
         out_shape=(
-            jax.ShapeDtypeStruct((local_rows, features), F32),
-            jax.ShapeDtypeStruct(square, BF16),
-            jax.ShapeDtypeStruct((out_block, features), F32),
+            pltpu.VMEM((local_rows, features), F32),
+            pltpu.VMEM((out_block, features), F32),
         ),
         in_specs=[hbm] * 12,
-        out_specs=(vmem, vmem, vmem),
+        out_specs=(vmem, vmem),
         scratch_shapes=scratch,
         compiler_params=pltpu.CompilerParams(
             collective_id=0, has_side_effects=True, vmem_limit_bytes=48 * 1024 * 1024
@@ -589,14 +600,18 @@
         )
     )
     mesh_grad, weight_grad = pl.pallas_call(
-        last_kernel,
+        write_out,
         out_shape=(
             jax.ShapeDtypeStruct((local_rows, features), F32),
             jax.ShapeDtypeStruct((out_block, features), F32),
         ),
-        in_specs=[vmem] * 3,
-        out_specs=(vmem, vmem),
-    )(row_grads, w_send_near, weight_grad)
+        in_specs=[vmem] * 2,
+        out_specs=(hbm, hbm),
+        scratch_shapes=[pltpu.SemaphoreType.DMA((2,))],
+    )(
+        pltpu.with_memory_space_constraint(mesh_grad, pltpu.VMEM),
+        pltpu.with_memory_space_constraint(weight_grad, pltpu.VMEM),
+    )
     return (mesh_grad[None], weight_grad)
 
 

time: 62.8 us -> 56.8 us (0.904)
  Pallas kernels: 59.9 us -> 56.1 us
  local copies, waits for them, and re-layouts: 2.09 us -> 0 us
    pallas_call x1, Pallas kernels: 57.7 us -> 55.3 us  [body(): pl.pallas_call(functools.partial(kernel, n_ens, n_sp, 1.0 / math.sqrt(tot...]
    unnamed x6 -> x0, local copies, waits for them, and re-layouts: 2.09 us -> none
    pallas_call x1, Pallas kernels: 2.29 us -> 0.72 us  [body(): pl.pallas_call(write_out, out_shape=(jax.ShapeDtypeStruct((local_rows, fe...]
where the time goes in v3:
time: 56.8 us; the launch traced here: 56.7 us
  Pallas kernels  56.1 us (99%)
  between operations  0.64 us (1%)
    pallas_call x1, Pallas kernels, body(): pl.pallas_call(functools.partial(kernel, n_ens, n_sp, 1.0 / math.sqrt(tot...  55.3 us

profile of v3, /device:TPU:1, one launch (start us, length us, event | category | flops | bytes accessed | tf_op | source)
XLA Modules:
  0.0 56.7 jit_solution(6930828748795484283)
XLA Ops:
  0.6 55.3 %shard_map.131 = (f32[128,512]{1,0:T(8,128)S(1)}, f32[16,512]{1,0:T(8,128)S(1)}) custom-call(bf16[128,512]{1,0:T(8,128)(2,1)} %bitcast.11, bf16[512,512]{1,0:T(8,128)(2,1)} %emb_h.1, bf16[512,512]{1,0:T(8,128)(2,1)} %w_send_h.1, bf16[512,512]{1,0:T(8,128)(2,1)} %w_recv_h.1, bf16[512,512]{1,0:T(8,128)(2,1)} %w_msg_h.1, bf16[512,512]{1,0:T(8,128)(2,1)} %w_node_h.1, ...), custom_call_target="tpu_custom_call" | custom-call | tf_op jit(solution)/shard_map/pallas_call | solution.py:571
  56.0 0.7 %shard_map.132 = (f32[128,512]{1,0:T(8,128)}, f32[16,512]{1,0:T(8,128)}) custom-call(f32[128,512]{1,0:T(8,128)S(1)} %get-tuple-element.6.mesh_in, f32[16,512]{1,0:T(8,128)S(1)} %get-tuple-element.7.weight_in), custom_call_target="tpu_custom_call" | custom-call | tf_op jit(solution)/shard_map/pallas_call | solution.py:602

commit v4 on v3

--- a/solution.py
+++ b/solution.py
@@ -50,10 +50,6 @@
 
 def wrap(i, n):
     return jnp.where(i < 0, i + n, jnp.where(i >= n, i - n, i))
-
-
-def from_far(t, n):
-    return n // 2 + (1 - 2 * lax.rem(t, 2)) * lax.div(t + 1, 2)
 
 
 def kernel(
@@ -144,23 +140,26 @@
     part_points = points // PARTS
     half = features // 2
 
-    def space_peer(t):
-        dy = from_far(lax.div(t, n_x), n_y)
-        dx = from_far(lax.rem(t, n_x), n_x)
-        to = lax.rem(y + dy, n_y) * n_x + lax.rem(x + dx, n_x)
-        back_place = lax.rem(n_y - dy, n_y) * n_x + lax.rem(n_x - dx, n_x)
-        return to, dy * n_x + dx, back_place
+    def hops(d, n):
+        return min(d, n - d)
+
+    rows_of_y = [lax.rem(y + dy, n_y) * n_x for dy in range(n_y)]
+    columns_of_x = [lax.rem(x + dx, n_x) for dx in range(n_x)]
+    offsets = [(dy, dx) for dy in range(n_y) for dx in range(n_x) if (dy, dx) != (0, 0)]
+    offsets.sort(key=lambda d: -hops(d[0], n_y) - hops(d[1], n_x))
+    space_peers = [
+        (rows_of_y[dy] + columns_of_x[dx], dy * n_x + dx, (n_y - dy) % n_y * n_x + (n_x - dx) % n_x)
+        for dy, dx in offsets
+    ]
+    ens_offsets = sorted(range(1, n_ens), key=lambda q: -hops(q // 2, n_ens // 2))
+    ens_peers = [(lax.rem(ens + q, n_ens), q) for q in ens_offsets]
 
     barrier = pltpu.get_barrier_semaphore()
 
-    @pl.loop(0, n_sp - 1)
-    def _(t):
-        to, _, _ = space_peer(t)
+    for to, _, _ in space_peers:
         pl.semaphore_signal(barrier, inc=1, device_id={"space": to}, device_id_type=MESH)
 
-    @pl.loop(0, n_ens - 1)
-    def _(t):
-        to = lax.rem(ens + from_far(t, n_ens), n_ens)
+    for to, _ in ens_peers:
         pl.semaphore_signal(barrier, inc=1, device_id={"ens": to}, device_id_type=MESH)
 
     loads = [
@@ -218,9 +217,7 @@
     pl.semaphore_wait(barrier, n_sp + n_ens - 2)
 
     def space_exchange(src, dst, which):
-        @pl.loop(0, n_sp - 1)
-        def _(t):
-            to, place, back_place = space_peer(t)
+        for to, place, back_place in space_peers:
             remote(src.at[place], dst.at[back_place], which, {"space": to}).start()
 
     space_exchange(out_rows, in_rows, 0)
@@ -301,10 +298,7 @@
 
         pred_in[h, 0] = pred[h, ens]
 
-        @pl.loop(0, n_ens - 1)
-        def _(t):
-            q = from_far(t, n_ens)
-            to = lax.rem(ens + q, n_ens)
+        for to, q in ens_peers:
             remote(pred.at[h, to], pred_in.at[h, n_ens - q], 1 + h, {"ens": to}).start()
 
     def slopes(h):
@@ -344,10 +338,7 @@
         grad_out[h] = grad_wide[...].astype(BF16)
         grad_in[h, 0] = grad_out[h, 0]
 
-        @pl.loop(0, n_ens - 1)
-        def _(t):
-            q = from_far(t, n_ens)
-            to = lax.rem(ens + q, n_ens)
+        for to, q in ens_peers:
             remote(
                 grad_out.at[h, q], grad_in.at[h, n_ens - q], 1 + PARTS + h, {"ens": to}
             ).start()
@@ -418,9 +409,7 @@
     sum_out[...] = blocks
     sum_in[0] = sum_out[sp]
 
-    @pl.loop(0, n_sp - 1)
-    def _(t):
-        to, _, back_place = space_peer(t)
+    for to, _, back_place in space_peers:
         remote(sum_out.at[to], sum_in.at[back_place], 5, {"space": to}).start()
 
     blocks = to_blocks(
@@ -434,10 +423,7 @@
     total_out[...] = jnp.sum(sum_in[...].astype(F32), axis=0).astype(BF16)
     total_in[0] = total_out[...]
 
-    @pl.loop(0, n_ens - 1)
-    def _(t):
-        q = from_far(t, n_ens)
-        to = lax.rem(ens + q, n_ens)
+    for to, q in ens_peers:
         remote(total_out, total_in.at[n_ens - q], 8, {"ens": to}).start()
 
     whole(rows_in.at[pl.ds(1, n_sp - 1)], 6).wait_recv()

time: 56.8 us -> 56.4 us (level)
  no operation moved by 1% of the time
where the time goes in v4:
time: 56.4 us; the launch traced here: 56.3 us
  Pallas kernels  55.6 us (99%)
  between operations  0.64 us (1%)
    pallas_call x1, Pallas kernels, body(): pl.pallas_call(functools.partial(kernel, n_ens, n_sp, 1.0 / math.sqrt(tot...  54.9 us

profile of v4, /device:TPU:1, one launch (start us, length us, event | category | flops | bytes accessed | tf_op | source)
XLA Modules:
  0.0 56.3 jit_solution(15216408007414152002)
XLA Ops:
  0.6 54.9 %shard_map.131 = (f32[128,512]{1,0:T(8,128)S(1)}, f32[16,512]{1,0:T(8,128)S(1)}) custom-call(bf16[128,512]{1,0:T(8,128)(2,1)} %bitcast.11, bf16[512,512]{1,0:T(8,128)(2,1)} %emb_h.1, bf16[512,512]{1,0:T(8,128)(2,1)} %w_send_h.1, bf16[512,512]{1,0:T(8,128)(2,1)} %w_recv_h.1, bf16[512,512]{1,0:T(8,128)(2,1)} %w_msg_h.1, bf16[512,512]{1,0:T(8,128)(2,1)} %w_node_h.1, ...), custom_call_target="tpu_custom_call" | custom-call | tf_op jit(solution)/shard_map/pallas_call | solution.py:557
  55.5 0.7 %shard_map.132 = (f32[128,512]{1,0:T(8,128)}, f32[16,512]{1,0:T(8,128)}) custom-call(f32[128,512]{1,0:T(8,128)S(1)} %get-tuple-element.6.mesh_in, f32[16,512]{1,0:T(8,128)S(1)} %get-tuple-element.7.weight_in), custom_call_target="tpu_custom_call" | custom-call | tf_op jit(solution)/shard_map/pallas_call | solution.py:588

commit v5 on v4

--- a/solution.py
+++ b/solution.py
@@ -17,13 +17,17 @@
 PARTS = 2
 
 
-def silu(u):
-    return u * jnp.tanh(u) + u
-
-
-def twice_slope(u):
-    t = jnp.tanh(u)
-    return 1.0 + t + u * (1.0 - t * t)
+def sigmoid(v):
+    return 1.0 / (1.0 + jnp.exp(-v))
+
+
+def silu(v):
+    return v * sigmoid(v)
+
+
+def slope(v):
+    s = sigmoid(v)
+    return s * (1.0 + v * (1.0 - s))
 
 
 def dot(a, b):
@@ -224,7 +228,7 @@
 
     loads[2].wait()
     loads[3].wait()
-    grid_proj[...] = 0.5 * dot(emb[...], w_recv[...])
+    grid_proj[...] = dot(emb[...], w_recv[...])
     pick_t[...] = jnp.transpose(pick_wide).astype(BF16)
     loads[4].wait()
     loads[5].wait()
@@ -280,20 +284,22 @@
             for n in range(0, features, 256):
                 lanes = pl.ds(n, 256)
                 base = grid_proj[rows, lanes]
-                total = jnp.zeros((128, 256), F32)
-                for k in range(per_point):
-                    u = dot(one_hot[k, rows, :], slot_proj[:, lanes]) + base
-                    pre[k, rows, lanes] = u
+                v = dot(one_hot[0, rows, :], slot_proj[:, lanes]) + base
+                pre[0, rows, lanes] = v
+                total = silu(v)
+                for k in range(1, per_point):
+                    v = dot(one_hot[k, rows, :], slot_proj[:, lanes]) + base
+                    pre[k, rows, lanes] = v
                     mask = jnp.concatenate([live[k, rows, :]] * 2, axis=1)
-                    total += silu(u) * mask
+                    total += silu(v) * mask
                 summed_act[rows, lanes] = total.astype(BF16)
 
         node_in = (
             dot(summed_act[span, :], w_msg[...]) + emb[span, :].astype(F32)
         ).astype(BF16)
-        u = 0.5 * dot(node_in, w_node[...])
-        node_pre[span, :] = u
-        hidden = silu(u).astype(BF16)
+        v = dot(node_in, w_node[...])
+        node_pre[span, :] = v
+        hidden = silu(v).astype(BF16)
         pred[h] = dot_t(hidden, w_out[...]).reshape(pred.shape[1:]).astype(BF16)
 
         pred_in[h, 0] = pred[h, ens]
@@ -307,8 +313,8 @@
             rows = rows_of(h, i)
             base = grid_proj[rows, :]
             for k in range(per_point):
-                pre[k, rows, :] = twice_slope(pre[k, rows, :])
-            node_pre[rows, :] = 0.5 * twice_slope(node_pre[rows, :])
+                pre[k, rows, :] = slope(pre[k, rows, :])
+            node_pre[rows, :] = slope(node_pre[rows, :])
 
     def scores(h):
         whole(pred_in.at[h, pl.ds(1, n_ens - 1)], 1 + h).wait_recv()
@@ -363,7 +369,7 @@
         @pl.loop(0, part_points // step)
         def _(i):
             rows = rows_of(h, i)
-            b = 0.5 * back[pl.ds(pl.multiple_of(i * step, step), step), :]
+            b = back[pl.ds(pl.multiple_of(i * step, step), step), :]
             for k in range(per_point):
                 pre_grad[
                     pl.ds(pl.multiple_of(k * part_points + i * step, step), step), :
@@ -371,7 +377,7 @@
 
     whole(in_rows.at[pl.ds(1, n_sp - 1)], 0).wait_recv()
     arrived = from_blocks(in_rows[...].astype(F32)).astype(BF16)
-    slot_proj[...] = (0.5 * dot(arrived, w_send[...])).astype(BF16)
+    slot_proj[...] = dot(arrived, w_send[...]).astype(BF16)
     for h in range(PARTS):
         forward(h)
 
@@ -387,23 +393,23 @@
     theirs, ours = 1 - core, core
     for h in range(PARTS - 1):
         edge_backward(h)
-        back[...] = dot_t(edge_grad[h], w_msg[...])
         for i, which in enumerate((theirs, ours)):
             term = weight_half(which, h)
             halves[i] = term if h == 0 else halves[i] + term
-        slot_backward(h)
-        term = dot(one_hot_t[h], pre_grad[...])
-        slot_grad[...] = term if h == 0 else slot_grad[...] + term
 
     last = PARTS - 1
     edge_backward(last)
     pair_out[...] = (halves[0] + weight_half(theirs, last)).astype(BF16)
     pair = remote(pair_out, pair_in, 7, {"ens": ens + 1 - 2 * core})
     pair.start()
-    back[...] = dot_t(edge_grad[last], w_msg[...])
     own = halves[1] + weight_half(ours, last)
     halves[1] = own
-    slot_backward(last)
+    for h in range(PARTS):
+        back[...] = dot_t(edge_grad[h], w_msg[...])
+        slot_backward(h)
+        if h < last:
+            term = dot(one_hot_t[h], pre_grad[...])
+            slot_grad[...] = term if h == 0 else slot_grad[...] + term
     pair.wait_recv()
     blocks = to_blocks(halves[1] + pair_in[...].astype(F32), n_sp).astype(BF16)
     sum_out[...] = blocks

time: 56.4 us -> 56.4 us (level)
  no operation moved by 1% of the time
where the time goes in v5:
time: 56.4 us; the launch traced here: 56.2 us
  Pallas kernels  55.6 us (99%)
  between operations  0.64 us (1%)
    pallas_call x1, Pallas kernels, body(): pl.pallas_call(functools.partial(kernel, n_ens, n_sp, 1.0 / math.sqrt(tot...  54.9 us

profile of v5, /device:TPU:1, one launch (start us, length us, event | category | flops | bytes accessed | tf_op | source)
XLA Modules:
  0.0 56.2 jit_solution(11825920507020639990)
XLA Ops:
  0.6 54.9 %shard_map.131 = (f32[128,512]{1,0:T(8,128)S(1)}, f32[16,512]{1,0:T(8,128)S(1)}) custom-call(bf16[128,512]{1,0:T(8,128)(2,1)} %bitcast.11, bf16[512,512]{1,0:T(8,128)(2,1)} %emb_h.1, bf16[512,512]{1,0:T(8,128)(2,1)} %w_send_h.1, bf16[512,512]{1,0:T(8,128)(2,1)} %w_recv_h.1, bf16[512,512]{1,0:T(8,128)(2,1)} %w_msg_h.1, bf16[512,512]{1,0:T(8,128)(2,1)} %w_node_h.1, ...), custom_call_target="tpu_custom_call" | custom-call | tf_op jit(solution)/shard_map/pallas_call | solution.py:563
  55.5 0.7 %shard_map.132 = (f32[128,512]{1,0:T(8,128)}, f32[16,512]{1,0:T(8,128)}) custom-call(f32[128,512]{1,0:T(8,128)S(1)} %get-tuple-element.6.mesh_in, f32[16,512]{1,0:T(8,128)S(1)} %get-tuple-element.7.weight_in), custom_call_target="tpu_custom_call" | custom-call | tf_op jit(solution)/shard_map/pallas_call | solution.py:594
